TPU v7x, 32 devices: a whole 2x2x4 slice. The times are simulated.
32 devices in a mesh: row: 4 (over y, core), col: 4 (over z), dp: 2 (over x).
Axes of the slice: x: 2, y: 2, z: 4, core: 2. Of those that a mesh axis runs over, the one named last changes fastest.
Arguments:
- pair: bfloat16 [2, 64, 512, 512], P('dp', None, 'row', 'col'), may hold values from -120 to 120
- cotangent: bfloat16 [2, 64, 512, 512], P('dp', None, 'row', 'col'), may hold values from -6 to 6
- chain: int32 [2, 512], P('dp'), may hold values from 0 to 3, never falling along the last dimension, each value on 1 to 256 neighbouring positions
- dilation: int32 [2], replicated, may hold values from 1 to 8, as said below
- w_one: bfloat16 [9, 64, 64], replicated, may hold values from -0.25 to 0.25
- w_two: bfloat16 [9, 64, 64], replicated, may hold values from -0.25 to 0.25
- gain_one: float32 [64], replicated, may hold values from 0.25 to 1.75
- gain_two: float32 [64], replicated, may hold values from 0.25 to 1.75
- inter_bias: float32 [64], replicated, may hold values from -4 to 4
Outputs:
- grad_w_one: float32 [9, 64, 64], replicated
- grad_w_two: float32 [9, 64, 64], replicated
- grad_gain_one: float32 [64], replicated
- grad_gain_two: float32 [64], replicated
- grad_inter: float32 [64], replicated
- loss: float32 [], replicated
Inputs may be any that keep to these rules, and one draw needn't show every extreme that they name: `dilation`: each entry is 1, 2, 4 or 8, and at least one entry is 8. chain numbers never fall along a complex's residues; each of the 4 chains has at most 256 residues.
All inputs are finite; a program needn't handle non-finite values.
Results may differ from a plain program's by a relative error of at most 0.0071.
Values may be sent and summed in bfloat16 or wider, within the bound.
A program may use at most 128 MiB of HBM per device.

v0:
```python
import jax
import jax.numpy as jnp
from jax import lax
from jax.sharding import PartitionSpec as P

kernel_reach = 8
eps = 1e-05


def padded(block, sides, width):
    for axis, dim in sides:
        count = lax.axis_size(axis)
        forward = [(i, i + 1) for i in range(count - 1)]
        backward = [(target, source) for source, target in forward]
        low = lax.ppermute(
            lax.slice_in_dim(block, block.shape[dim] - width, None, axis=dim), axis, forward
        )
        high = lax.ppermute(lax.slice_in_dim(block, 0, width, axis=dim), axis, backward)
        block = jnp.concatenate([low, block, high], axis=dim)
    return block


def elu(z):
    return jnp.where(z > 0, z, jnp.exp(jnp.minimum(z, 0.0)) - 1.0)


def elu_slope(z):
    return jnp.where(z > 0, 1.0, jnp.exp(jnp.minimum(z, 0.0)))


def kernel_tap_window(padded_input, first, second, input_shape):
    zero = jnp.int32(0)
    return lax.dynamic_slice(padded_input, (zero, first, second), input_shape)


def widen(values):
    return padded(values, (("row", 1), ("col", 2)), kernel_reach)


def dilated_convolve(padded_input, input_shape, kernel_weights, dilation_rate):
    chans = input_shape[0]
    total = jnp.zeros((chans, input_shape[1] * input_shape[2]), jnp.float32)
    for step in range(9):
        upper_triangle, left_padding = (step // 3 - 1, step % 3 - 1)
        window_slice = kernel_tap_window(
            padded_input,
            kernel_reach + dilation_rate * upper_triangle,
            kernel_reach + dilation_rate * left_padding,
            input_shape,
        )
        total = total + jnp.dot(
            kernel_weights[step],
            window_slice.reshape(chans, -1),
            preferred_element_type=jnp.float32,
        )
    return total.reshape(input_shape)


def convolve_backward(output_gradient, kernel_weights, dilation_rate):
    chans = output_gradient.shape[0]
    padded_input = widen(output_gradient)
    total = jnp.zeros((chans, output_gradient.shape[1] * output_gradient.shape[2]), jnp.float32)
    for step in range(9):
        upper_triangle, left_padding = (step // 3 - 1, step % 3 - 1)
        window_slice = kernel_tap_window(
            padded_input,
            kernel_reach - dilation_rate * upper_triangle,
            kernel_reach - dilation_rate * left_padding,
            output_gradient.shape,
        )
        total = total + jnp.dot(
            kernel_weights[step].T,
            window_slice.reshape(chans, -1),
            preferred_element_type=jnp.float32,
        )
    return total.reshape(output_gradient.shape)


def kernel_weight_gradient(output_gradient, padded_input, dilation_rate):
    chans = output_gradient.shape[0]
    flat = output_gradient.reshape(chans, -1)
    result = []
    for step in range(9):
        upper_triangle, left_padding = (step // 3 - 1, step % 3 - 1)
        window_slice = kernel_tap_window(
            padded_input,
            kernel_reach + dilation_rate * upper_triangle,
            kernel_reach + dilation_rate * left_padding,
            output_gradient.shape,
        )
        result.append(
            lax.dot_general(
                flat,
                window_slice.reshape(chans, -1),
                (((1,), (1,)), ((), ())),
                preferred_element_type=jnp.float32,
            )
        )
    return jnp.stack(result)


def paired_total(first, second):
    return lax.psum((first, second), ("row", "col"))


def normalize(values, count):
    totals = paired_total(jnp.sum(values, axis=(1, 2)), jnp.sum(values * values, axis=(1, 2)))
    mean = totals[0] / count
    var = totals[1] / count - mean * mean
    centred = values - mean[:, None, None]
    return (centred * lax.rsqrt(var + eps)[:, None, None], var)


def local(pair, cotangent, chain, dilation, w_one, w_two, gain_one, gain_two, inter_bias):
    chans, side = (pair.shape[1], pair.shape[2])
    groups = lax.axis_size("row")
    length = side * groups
    count = float(length * length)
    stacked = pair.reshape(1, 1, chans, side, side)
    sectioned = lax.all_to_all(
        lax.all_to_all(stacked, "row", split_axis=3, concat_axis=0, tiled=True),
        "col",
        split_axis=0,
        concat_axis=1,
        tiled=True,
    )
    landed = lax.all_to_all(sectioned, "row", split_axis=1, concat_axis=0, tiled=True)
    pieces = landed.reshape(groups, chans, side // groups, side)
    mirrored = jnp.swapaxes(jnp.transpose(pieces, (1, 0, 2, 3)).reshape(chans, side, side), 1, 2)
    tile = pair[0]
    sym = ((tile.astype(jnp.float32) + mirrored.astype(jnp.float32)) * 0.5).astype(jnp.bfloat16)
    wide = sym.astype(jnp.float32)
    norm_one, var_one = normalize(wide, count)
    z_one = gain_one[:, None, None] * norm_one
    act_one = elu(z_one).astype(jnp.bfloat16)
    row_ids = lax.dynamic_slice_in_dim(chain[0], lax.axis_index("row") * side, side)
    col_ids = lax.dynamic_slice_in_dim(chain[0], lax.axis_index("col") * side, side)
    cross = (row_ids[:, None] != col_ids[None, :]).astype(jnp.float32)
    padded_one = widen(act_one)
    hid = (
        dilated_convolve(padded_one, act_one.shape, w_one, dilation[0])
        + inter_bias[:, None, None] * cross[None]
    )
    norm_two, var_two = normalize(hid, count)
    z_two = gain_two[:, None, None] * norm_two
    act_two = elu(z_two).astype(jnp.bfloat16)
    padded_two = widen(act_two)
    upd = dilated_convolve(padded_two, act_two.shape, w_two, dilation[1])
    cot_wide = cotangent[0].astype(jnp.float32)
    loss = jnp.sum((wide + upd) * cot_wide) / length
    g_upd = (cot_wide / length).astype(jnp.bfloat16)
    grad_two = kernel_weight_gradient(g_upd, padded_two, dilation[1])
    d_act_two = convolve_backward(g_upd, w_two, dilation[1])
    d_z_two = d_act_two * elu_slope(z_two)
    grad_g_two = jnp.sum(d_z_two * norm_two, axis=(1, 2))
    d_norm_two = d_z_two * gain_two[:, None, None]
    sums = paired_total(
        jnp.sum(d_norm_two, axis=(1, 2)), jnp.sum(d_norm_two * norm_two, axis=(1, 2))
    )
    mean_a = sums[0] / count
    mean_b = sums[1] / count
    d_hid = (d_norm_two - mean_a[:, None, None] - norm_two * mean_b[:, None, None]) * lax.rsqrt(
        var_two + eps
    )[:, None, None]
    grad_int = jnp.sum(d_hid * cross[None], axis=(1, 2))
    d_hid_low = d_hid.astype(jnp.bfloat16)
    grad_one = kernel_weight_gradient(d_hid_low, padded_one, dilation[0])
    d_act_one = convolve_backward(d_hid_low, w_one, dilation[0])
    grad_g_one = jnp.sum(d_act_one * elu_slope(z_one) * norm_one, axis=(1, 2))
    totals = lax.psum(
        (grad_one, grad_two, grad_g_one, grad_g_two, grad_int, loss), ("row", "col", "dp")
    )
    return (totals[0], totals[1], totals[2], totals[3], totals[4], totals[5])


def solution(mesh):
    in_specs = (
        P("dp", None, "row", "col"),
        P("dp", None, "row", "col"),
        P("dp", None),
        P(),
        P(),
        P(),
        P(),
        P(),
        P(),
    )
    out_specs = (P(), P(), P(), P(), P(), P())
    return jax.shard_map(local, mesh=mesh, in_specs=in_specs, out_specs=out_specs, check_vma=False)
```

profile of v0, /device:TPU:0, one launch (start us, length us, event | category | flops | bytes accessed | tf_op | source)
XLA Modules:
  0.0 701.5 jit_solution(5183082801833041562)
XLA Ops:
  7.2 4.3 copy.340
  11.5 4.6 all-to-all-start
  20.3 3.0 collective-permute-start
  23.6 18.8 %all-to-all-done = bf16[1,1,64,128,128]{4,2,1,0,3:T(8,128)(2,1)} async-done(((bf16[1,1,64,128,128]{4,2,1,0,3:T(8,128)(2,1)}), bf16[1,1,64,128,128]{4,2,1,0,3:T(8,128)(2,1)}, u32[]{:S(2)}, u32[]{:S(2)}) %all-to-all-start) | async-done | bytes 2097184 | tf_op jit(solution)/shard_map/all_to_all | solution.py:121
  42.4 4.3 copy.339
  46.7 5.8 all-to-all-start.1
  52.6 4.3 fusion.4
  63.9 4.3 copy.72
  68.6 3.4 fusion.361
  72.0 3.9 copy.65
  77.3 3.9 copy.64
  81.2 5.3 collective-permute-start.2
  86.6 4.2 copy.67
  91.9 5.0 copy.66
  96.9 8.6 %pad_maximum_fusion = bf16[64,144,144]{2,0,1:T(8,128)(2,1)} fusion(bf16[64,144,8]{2,0,1:T(8,128)(2,1)} %copy.67, bf16[64,8,128]{2,0,1:T(8,128)(2,1)S(1)} %collective-permute-done.1, bf16[64,128,128]{2,0,1:T(8,128)(2,1)S(1)} %fusion.2, bf16[64,8,128]{2,0,1:T(8,128)(2,1)S(1)} %collective-permute-done, bf16[64,144,8]{2,0,1:T(8,128)(2,1)} %copy.66), kind=kLoop, calls=%fused_computation.46 | loop fusion | flops 13271040 | bytes 5308416 | tf_op jit(solution)/shard_map/concatenate | solution.py:19
  105.5 21.0 %dynamic-slice_bitcast_fusion.8 = (bf16[128,8,8,128]{3,2,1,0:T(8,128)(2,1)}, bf16[128,8,8,128]{3,2,1,0:T(8,128)(2,1)}, bf16[128,8,8,128]{3,2,1,0:T(8,128)(2,1)},...) fusion(bf16[64,144,144]{2,0,1:T(8,128)(2,1)} %pad_maximum_fusio, ...), kind=kLoop, calls=%fused_computation.182 | loop fusion | bytes 33554440
  130.9 4.6 all-to-all-start.2
  135.7 3.1 convolution_add_fusion.30
  145.0 16.3 %all-to-all-done.2 = bf16[1,4,64,32,128]{4,3,2,0,1:T(8,128)(2,1)} async-done(((bf16[1,4,64,32,128]{4,3,2,0,1:T(8,128)(2,1)}), bf16[1,4,64,32,128]{4,3,2,0,1:T(8,128)(2,1)}, u32[]{:S(2)}, u32[]{:S(2)}) %all-to-all-start.2) | async-done | bytes 2097184 | tf_op jit(solution)/shard_map/all_to_all | solution.py:127
  161.2 4.1 bitcast_convert_fusion
  165.4 5.5 copy.82
  170.9 5.2 convert_reduce_fusion
  176.1 48.7 %all-reduce.4 = (f32[64]{0:T(128)S(1)}, f32[64]{0:T(128)S(1)}) all-reduce(f32[64]{0:T(128)S(1)} %get-tuple-element.14, f32[64]{0:T(128)S(1)} %get-tuple-element.13), channel_id=1, replica_groups=mesh['row'=4,'col'=4,'dp'=2] {'row','col'}, use_global_device_ids=true, to_apply=%region_3.0 | all-reduce | flops 128 | bytes 1024 | tf_op jit(solution)/shard_map/psum | solution.py:103
  224.8 3.3 fusion.5
  232.5 4.3 convolution_add_fusion.26
  237.1 3.3 fusion.360
  240.4 3.9 copy.84
  245.9 3.9 copy.83
  249.8 5.3 collective-permute-start.6
  255.1 5.5 convolution_add_fusion.25
  260.6 4.1 copy.86
  264.8 5.0 copy.85
  269.8 8.6 %pad_maximum_fusion.1 = bf16[64,144,144]{2,0,1:T(8,128)(2,1)} fusion(bf16[64,144,8]{2,0,1:T(8,128)(2,1)} %copy.86, bf16[64,8,128]{2,0,1:T(8,128)(2,1)S(1)} %collective-permute-done.5, bf16[64,128,128]{2,0,1:T(8,128)(2,1)S(1)} %fusion.5, bf16[64,8,128]{2,0,1:T(8,128)(2,1)S(1)} %collective-permute-done.4, bf16[64,144,8]{2,0,1:T(8,128)(2,1)} %copy.85), kind=kLoop, calls=%fused_computation.47 | loop fusion | flops 13271040 | bytes 5308416 | tf_op jit(solution)/shard_map/concatenate | solution.py:19
  278.4 20.6 %dynamic-slice_bitcast_fusion.22 = (bf16[128,8,8,128]{3,2,1,0:T(8,128)(2,1)}, bf16[128,8,8,128]{3,2,1,0:T(8,128)(2,1)S(1)}, bf16[128,8,8,128]{3,2,1,0:T(8,128)(2...) fusion(bf16[64,144,144]{2,0,1:T(8,128)(2,1)} %pad_maximum_fusio, ...), kind=kLoop, calls=%fused_computation.211 | loop fusion | bytes 33554440
  312.4 3.4 fusion.28
  315.7 29.7 %all-reduce.3 = (f32[64]{0:T(128)S(1)}, f32[64]{0:T(128)S(1)}) all-reduce(f32[64]{0:T(128)S(1)} %get-tuple-element.10, f32[64]{0:T(128)S(1)} %get-tuple-element.9), channel_id=1, replica_groups=mesh['row'=4,'col'=4,'dp'=2] {'row','col'}, use_global_device_ids=true, to_apply=%region_7.8 | all-reduce | flops 128 | bytes 1024 | tf_op jit(solution)/shard_map/psum | solution.py:103
  345.4 7.1 %multiply_reduce_fusion.1 = (f32[64]{0:T(128)}, f32[64]{0:T(128)S(1)}, f32[64]{0:T(128)S(1)}, f32[16384,64]{0,1:T(8,128)}) fusion(f32[64]{0:T(128)S(1)} %copy-done.51, f32[64]{0:T(128)S(1)} %get-tuple-element.84, f32[64]{0:T(128)S(1)} %get-tuple-element.83, f32[16384]{0:T(1024)S(1)} %fusion.247, f32[64]{0:T(128)S(1)} %copy-done.48, ...), kind=kOutput, calls=%fused_computation.80 | convolution fusion | flops 150994752 | bytes 14764800 | tf_op jit(solution)/shard_map/dot_general | solution.py:71
  352.5 32.1 %all-reduce.2 = (f32[64]{0:T(128)S(1)}, f32[64]{0:T(128)S(1)}) all-reduce(f32[64]{0:T(128)S(1)} %get-tuple-element.8, f32[64]{0:T(128)S(1)} %get-tuple-element.7), channel_id=1, replica_groups=mesh['row'=4,'col'=4,'dp'=2] {'row','col'}, use_global_device_ids=true, to_apply=%region_11.12 | all-reduce | flops 128 | bytes 1024 | tf_op jit(solution)/shard_map/psum | solution.py:103
  384.6 7.4 %multiply_reduce_fusion = (f32[64]{0:T(128)}, bf16[64,16384]{1,0:T(8,128)(2,1)}, bf16[8,128,8,128]{3,2,1,0:T(8,128)(2,1)}) fusion(f32[16384]{0:T(1024)S(1)} %fusion.247, f32[64]{0:T(128)S(1)} %get-tuple-element.91, f32[64]{0:T(128)S(1)} %get-tuple-element.92, f32[64]{0:T(128)S(1)} %get-tuple-element.84, f32[64]{0:T(128)S(1)} %get-tuple-element.83, ...), kind=kLoop, calls=%fused_computation.79 | loop fusion | flops 20971456 | bytes 12650240 | tf_op jit(solution)/shard_map/reduce_sum | solution.py:165
  405.2 3.0 collective-permute-start.8
  409.5 3.4 collective-permute-start.12
  413.3 3.3 fusion.359
  416.6 4.6 copy.99
  422.4 4.6 copy.98
  427.0 5.2 collective-permute-start.10
  432.6 3.3 fusion.358
  435.8 3.9 copy.104
  441.0 4.6 copy.103
  445.6 5.4 collective-permute-start.14
  451.0 5.0 copy.101
  456.0 5.0 copy.100
  461.0 7.7 %pad_maximum_fusion.2 = bf16[64,144,144]{2,0,1:T(8,128)(2,1)S(1)} fusion(bf16[64,144,8]{2,0,1:T(8,128)(2,1)} %copy.101, bf16[64,8,128]{2,0,1:T(8,128)(2,1)S(1)} %collective-permute-done.9, bf16[64,128,128]{2,0,1:T(8,128)(2,1)} %copy-done.7, bf16[64,8,128]{2,0,1:T(8,128)(2,1)S(1)} %collective-permute-done.8, bf16[64,144,8]{2,0,1:T(8,128)(2,1)} %copy.100), kind=kLoop, calls=%fused_computation.48 | loop fusion | flops 13271040 | bytes 5308416 | tf_op jit(solution)/shard_map/concatenate | solution.py:19
  472.7 21.5 %dynamic-slice_bitcast_fusion.16 = (bf16[128,8,8,128]{3,2,1,0:T(8,128)(2,1)}, bf16[128,8,8,128]{3,2,1,0:T(8,128)(2,1)}, bf16[128,8,8,128]{3,2,1,0:T(8,128)(2,1)}...) fusion(bf16[64,144,144]{2,0,1:T(8,128)(2,1)} %copy-done, ...), kind=kLoop, calls=%fused_computation.191 | loop fusion | bytes 33554440
  494.2 4.7 fusion.155
  499.0 3.5 fusion.215
  517.2 4.4 convolution_add_fusion.4
  523.5 4.2 copy.106
  527.7 5.0 copy.105
  532.7 8.6 %pad_maximum_fusion.3 = bf16[64,144,144]{2,0,1:T(8,128)(2,1)} fusion(bf16[64,144,8]{2,0,1:T(8,128)(2,1)} %copy.106, bf16[64,8,128]{2,0,1:T(8,128)(2,1)S(1)} %collective-permute-done.13, bf16[64,128,128]{2,0,1:T(8,128)(2,1)S(1)} %get-tuple-element.64, bf16[64,8,128]{2,0,1:T(8,128)(2,1)S(1)} %collective-permute-done.12, bf16[64,144,8]{2,0,1:T(8,128)(2,1)} %copy.105), kind=kLoop, calls=%fused_computation.49 | loop fusion | flops 13271040 | bytes 5308416 | tf_op jit(solution)/shard_map/concatenate | solution.py:19
  541.3 21.0 %dynamic-slice_bitcast_fusion = (bf16[128,8,8,128]{3,2,1,0:T(8,128)(2,1)}, bf16[128,8,8,128]{3,2,1,0:T(8,128)(2,1)}, bf16[128,8,8,128]{3,2,1,0:T(8,128)(2,1)}, b...) fusion(bf16[64,144,144]{2,0,1:T(8,128)(2,1)} %pad_maximum_fusio, ...), kind=kLoop, calls=%fused_computation.173 | loop fusion | bytes 33554440
  565.1 3.6 convolution_add_fusion.3
  588.3 3.4 fusion.3
  592.4 37.8 %all-reduce = (f32[64]{0:T(128)}, f32[64]{0:T(128)}, f32[64]{0:T(128)}, f32[]{:T(128)}) all-reduce(f32[64]{0:T(128)S(1)} %get-tuple-element.12, f32[64]{0:T(128)S(1)} %copy-done.58, f32[64]{0:T(128)S(1)} %copy-done.55, f32[]{:T(128)S(6)} %div.41), channel_id=1, replica_groups=mesh['row'=4,'col'=4,'dp'=2] {'row','col','dp'}, use_global_device_ids=true, to_apply=%region_15.16 | all-reduce | flops 193 | bytes 1544 | tf_op jit(solution)/shard_map/psum | solution.py:170
  630.3 60.8 %all-reduce.7.cloned.1.call-done = (f32[9,64,64]{2,1,0:T(8,128)}, f32[9,64,64]{2,1,0:T(8,128)}) async-done(((f32[9,64,64]{2,1,0:T(8,128)}, f32[9,64,64]{2,1,0:T(8,128)}), (f32[9,64,64]{2,1,0:T(8,128)}, f32[9,64,64]{2,1,0:T(8,128)})) %all-reduce.7.cloned.1.call-update) | async-done | bytes 294928 | tf_op jit(solution)/shard_map/psum | solution.py:170
  (216 shorter events, 101.9 us)
Async XLA Ops:
  11.5 11.9 %copy-start.57 = (s32[1,512]{1,0:T(1,128)S(1)}, s32[1,512]{1,0:T(1,128)}, u32[]{:S(2)}) copy-start(s32[1,512]{1,0:T(1,128)} %param.11) | copy-start | bytes 6148
  11.5 31.0 %all-to-all-start = ((bf16[1,1,64,128,128]{4,2,1,0,3:T(8,128)(2,1)}), bf16[1,1,64,128,128]{4,2,1,0,3:T(8,128)(2,1)}, u32[]{:S(2)}, u32[]{:S(2)}) async-start(bf16[1,1,64,128,128]{4,2,1,0,3:T(8,128)(2,1)} %bitcast.515), calls=%async_computation | async-start | bytes 4194304 | tf_op jit(solution)/shard_map/all_to_all | solution.py:121
  19.0 49.2 %collective-permute-start.1 = (bf16[64,8,128]{2,0,1:T(8,128)(2,1)S(1)}, bf16[64,8,128]{2,0,1:T(8,128)(2,1)S(1)}, u32[]{:S(2)}, u32[]{:S(2)}) collective-permute-start(bf16[64,8,128]{2,0,1:T(8,128)(2,1)S(1)} %get-tuple-element.80), channel_id=1, source_target_pairs={{8,0},{16,8},{24,16},{9,1},{17,9},{25,17},{10,2},{18,10},{26,18},{... | collective-permute-start | bytes 393224 | tf_op jit(solution)/shard_map/ppermute | solution.py:18
  20.3 47.9 %collective-permute-start = (bf16[64,8,128]{2,0,1:T(8,128)(2,1)S(1)}, bf16[64,8,128]{2,0,1:T(8,128)(2,1)S(1)}, u32[]{:S(2)}, u32[]{:S(2)}) collective-permute-start(bf16[64,8,128]{2,0,1:T(8,128)(2,1)S(1)} %get-tuple-element.79), channel_id=1, source_target_pairs={{0,8},{8,16},{16,24},{1,9},{9,17},{17,25},{2,10},{10,18},{18,26},{... | collective-permute-start | bytes 393224 | tf_op jit(solution)/shard_map/ppermute | solution.py:15
  46.7 10.1 %copy-start.56 = (s32[2]{0:T(128)S(1)}, s32[2]{0:T(128)}, u32[]{:S(2)}) copy-start(s32[2]{0:T(128)} %param.12) | copy-start | bytes 28
  46.7 84.1 %all-to-all-start.1 = ((bf16[4,1,64,32,128]{4,3,2,1,0:T(8,128)(2,1)}), bf16[4,1,64,32,128]{4,3,2,1,0:T(8,128)(2,1)}, u32[]{:S(2)}, u32[]{:S(2)}) async-start(bf16[4,1,64,32,128]{4,3,2,1,0:T(8,128)(2,1)} %bitcast.520), calls=%async_computation.1 | async-start | bytes 4194304 | tf_op jit(solution)/shard_map/all_to_all | solution.py:120
  75.9 10.7 %collective-permute-start.3 = (bf16[64,144,8]{1,2,0:T(8,128)(2,1)S(1)}, bf16[64,144,8]{1,2,0:T(8,128)(2,1)S(1)}, u32[]{:S(2)}, u32[]{:S(2)}) collective-permute-start(bf16[64,144,8]{1,2,0:T(8,128)(2,1)S(1)} %copy.65), channel_id=1, source_target_pairs={{2,0},{4,2},{6,4},{3,1},{5,3},{7,5},{10,8},{12,10},{14,12},{11,9},... | collective-permute-start | bytes 442376 | tf_op jit(solution)/shard_map/ppermute | solution.py:18
  81.2 10.7 %collective-permute-start.2 = (bf16[64,144,8]{1,2,0:T(8,128)(2,1)S(1)}, bf16[64,144,8]{1,2,0:T(8,128)(2,1)}, u32[]{:S(2)}, u32[]{:S(2)}) collective-permute-start(bf16[64,144,8]{1,2,0:T(8,128)(2,1)S(1)} %copy.64), channel_id=1, source_target_pairs={{0,2},{2,4},{4,6},{1,3},{3,5},{5,7},{8,10},{10,12},{12,14},{9,11},... | collective-permute-start | bytes 442376 | tf_op jit(solution)/shard_map/ppermute | solution.py:15
  105.5 21.0 %copy-start.44 = (bf16[9,64,64]{2,1,0:T(8,128)(2,1)S(1)}, bf16[9,64,64]{2,1,0:T(8,128)(2,1)}, u32[]{:S(2)}) copy-start(bf16[9,64,64]{2,1,0:T(8,128)(2,1)} %param.14) | copy-start | bytes 221188
  130.9 4.9 copy-start.29
  130.9 30.3 %all-to-all-start.2 = ((bf16[1,4,64,32,128]{4,3,2,0,1:T(8,128)(2,1)}), bf16[1,4,64,32,128]{4,3,2,0,1:T(8,128)(2,1)}, u32[]{:S(2)}, u32[]{:S(2)}) async-start(bf16[1,4,64,32,128]{4,3,2,0,1:T(8,128)(2,1)} %bitcast.21), calls=%async_computation.2 | async-start | bytes 4194304 | tf_op jit(solution)/shard_map/all_to_all | solution.py:127
  135.5 555.6 %all-reduce.7.cloned.1.call-start = ((), (), s32[]{:S(2)}) async-start(), calls=%async_computation.3 | async-start | bytes 1179648 | tf_op jit(solution)/shard_map/psum | solution.py:170
  135.7 3.1 copy-start.27
  140.4 1.7 copy-start.26
  165.4 5.5 copy-start.39
  170.9 53.9 %copy-start.53 = (f32[64]{0:T(128)S(1)}, f32[64]{0:T(128)}, u32[]{:S(2)}) copy-start(f32[64]{0:T(128)} %param.15) | copy-start | bytes 772
  224.7 7.7 %copy-start.14 = (f32[16384,64]{0,1:T(8,128)S(1)}, f32[16384,64]{0,1:T(8,128)}, u32[]{:S(2)}) copy-start(f32[16384,64]{0,1:T(8,128)} %convolution_add_fusion.27) | copy-start | bytes 12582916
  224.8 80.6 %copy-start.49 = (f32[64]{0:T(128)}, f32[64]{0:T(128)S(1)}, u32[]{:S(2)}) copy-start(f32[64]{0:T(128)S(1)} %get-tuple-element.88) | copy-start | bytes 772
  228.1 41.7 %copy-start.4 = (bf16[64,128,128]{2,0,1:T(8,128)(2,1)}, bf16[64,128,128]{2,0,1:T(8,128)(2,1)S(1)}, u32[]{:S(2)}) copy-start(bf16[64,128,128]{2,0,1:T(8,128)(2,1)S(1)} %fusion.5) | copy-start | bytes 6291460
  228.1 8.7 %collective-permute-start.5 = (bf16[64,8,128]{2,0,1:T(8,128)(2,1)S(1)}, bf16[64,8,128]{2,0,1:T(8,128)(2,1)S(1)}, u32[]{:S(2)}, u32[]{:S(2)}) collective-permute-start(bf16[64,8,128]{2,0,1:T(8,128)(2,1)S(1)} %get-tuple-element.78), channel_id=1, source_target_pairs={{8,0},{16,8},{24,16},{9,1},{17,9},{25,17},{10,2},{18,10},{26,18},{... | collective-permute-start | bytes 393224 | tf_op jit(solution)/shard_map/ppermute | solution.py:18
  229.4 7.4 %collective-permute-start.4 = (bf16[64,8,128]{2,0,1:T(8,128)(2,1)S(1)}, bf16[64,8,128]{2,0,1:T(8,128)(2,1)S(1)}, u32[]{:S(2)}, u32[]{:S(2)}) collective-permute-start(bf16[64,8,128]{2,0,1:T(8,128)(2,1)S(1)} %get-tuple-element.77), channel_id=1, source_target_pairs={{0,8},{8,16},{16,24},{1,9},{9,17},{17,25},{2,10},{10,18},{18,26},{... | collective-permute-start | bytes 393224 | tf_op jit(solution)/shard_map/ppermute | solution.py:15
  244.2 16.4 %collective-permute-start.7 = (bf16[64,144,8]{1,2,0:T(8,128)(2,1)S(1)}, bf16[64,144,8]{1,2,0:T(8,128)(2,1)S(1)}, u32[]{:S(2)}, u32[]{:S(2)}) collective-permute-start(bf16[64,144,8]{1,2,0:T(8,128)(2,1)S(1)} %copy.84), channel_id=1, source_target_pairs={{2,0},{4,2},{6,4},{3,1},{5,3},{7,5},{10,8},{12,10},{14,12},{11,9},... | collective-permute-start | bytes 442376 | tf_op jit(solution)/shard_map/ppermute | solution.py:18
  249.8 14.9 %collective-permute-start.6 = (bf16[64,144,8]{1,2,0:T(8,128)(2,1)S(1)}, bf16[64,144,8]{1,2,0:T(8,128)(2,1)}, u32[]{:S(2)}, u32[]{:S(2)}) collective-permute-start(bf16[64,144,8]{1,2,0:T(8,128)(2,1)S(1)} %copy.83), channel_id=1, source_target_pairs={{0,2},{2,4},{4,6},{1,3},{3,5},{5,7},{8,10},{10,12},{12,14},{9,11},... | collective-permute-start | bytes 442376 | tf_op jit(solution)/shard_map/ppermute | solution.py:15
  278.4 20.6 %copy-start.45 = (bf16[9,64,64]{2,1,0:T(8,128)(2,1)S(1)}, bf16[9,64,64]{2,1,0:T(8,128)(2,1)}, u32[]{:S(2)}) copy-start(bf16[9,64,64]{2,1,0:T(8,128)(2,1)} %param.13) | copy-start | bytes 221188
  299.0 2.4 copy-start.38
  306.3 2.2 copy-start.34
  312.4 33.1 %copy-start.42 = (bf16[128,8,8,128]{3,2,1,0:T(8,128)(2,1)S(1)}, bf16[128,8,8,128]{3,2,1,0:T(8,128)(2,1)}, u32[]{:S(2)}) copy-start(bf16[128,8,8,128]{3,2,1,0:T(8,128)(2,1)} %get-tuple-element.54) | copy-start | bytes 6291460
  312.4 33.1 %copy-start.51 = (f32[64]{0:T(128)S(1)}, f32[64]{0:T(128)}, u32[]{:S(2)}) copy-start(f32[64]{0:T(128)} %param.16) | copy-start | bytes 772
  384.6 7.4 %copy-start.2 = (f32[16384,64]{0,1:T(8,128)S(1)}, f32[16384,64]{0,1:T(8,128)}, u32[]{:S(2)}) copy-start(f32[16384,64]{0,1:T(8,128)} %get-tuple-element.89) | copy-start | bytes 12582916
  384.6 7.4 %copy-start.15 = (f32[16384,64]{0,1:T(8,128)S(1)}, f32[16384,64]{0,1:T(8,128)}, u32[]{:S(2)}) copy-start(f32[16384,64]{0,1:T(8,128)} %get-tuple-element.90) | copy-start | bytes 12582916
  384.6 10.4 %slice-start = ((s8[4718592]{0:T(1024)(128)(4,1)}), s8[524288]{0:T(1024)(128)(4,1)S(1)}, s32[]{:S(2)}) async-start(s8[4718592]{0:T(1024)(128)(4,1)} %bitcast.516), calls=%async_computation.4 | async-start | bytes 1048576
  392.0 3.0 slice-start.1
  395.0 18.0 %copy-start.7 = (bf16[64,128,128]{2,0,1:T(8,128)(2,1)}, bf16[64,128,128]{2,0,1:T(8,128)(2,1)S(1)}, u32[]{:S(2)}) copy-start(bf16[64,128,128]{2,0,1:T(8,128)(2,1)S(1)} %get-tuple-element.63) | copy-start | bytes 6291460
  397.0 2.0 copy-start.5
  403.8 12.8 %copy-start.46 = (f32[9,64,64]{2,1,0:T(8,128)}, f32[9,64,64]{2,1,0:T(8,128)S(1)}, u32[]{:S(2)}) copy-start(f32[9,64,64]{2,1,0:T(8,128)S(1)} %fusion.197) | copy-start | bytes 442372
  403.9 9.1 %collective-permute-start.9 = (bf16[64,8,128]{2,0,1:T(8,128)(2,1)S(1)}, bf16[64,8,128]{2,0,1:T(8,128)(2,1)S(1)}, u32[]{:S(2)}, u32[]{:S(2)}) collective-permute-start(bf16[64,8,128]{2,0,1:T(8,128)(2,1)S(1)} %get-tuple-element.76), channel_id=1, source_target_pairs={{8,0},{16,8},{24,16},{9,1},{17,9},{25,17},{10,2},{18,10},{26,18},{... | collective-permute-start | bytes 393224 | tf_op jit(solution)/shard_map/ppermute | solution.py:18
  405.2 7.8 %collective-permute-start.8 = (bf16[64,8,128]{2,0,1:T(8,128)(2,1)S(1)}, bf16[64,8,128]{2,0,1:T(8,128)(2,1)S(1)}, u32[]{:S(2)}, u32[]{:S(2)}) collective-permute-start(bf16[64,8,128]{2,0,1:T(8,128)(2,1)S(1)} %get-tuple-element.75), channel_id=1, source_target_pairs={{0,8},{8,16},{16,24},{1,9},{9,17},{17,25},{2,10},{10,18},{18,26},{... | collective-permute-start | bytes 393224 | tf_op jit(solution)/shard_map/ppermute | solution.py:15
  408.2 24.0 %collective-permute-start.13 = (bf16[64,8,128]{2,0,1:T(8,128)(2,1)S(1)}, bf16[64,8,128]{2,0,1:T(8,128)(2,1)S(1)}, u32[]{:S(2)}, u32[]{:S(2)}) collective-permute-start(bf16[64,8,128]{2,0,1:T(8,128)(2,1)S(1)} %get-tuple-element.74), channel_id=1, source_target_pairs={{8,0},{16,8},{24,16},{9,1},{17,9},{25,17},{10,2},{18,10},{26,18},{... | collective-permute-start | bytes 393224 | tf_op jit(solution)/shard_map/ppermute | solution.py:18
  409.5 22.7 %collective-permute-start.12 = (bf16[64,8,128]{2,0,1:T(8,128)(2,1)S(1)}, bf16[64,8,128]{2,0,1:T(8,128)(2,1)S(1)}, u32[]{:S(2)}, u32[]{:S(2)}) collective-permute-start(bf16[64,8,128]{2,0,1:T(8,128)(2,1)S(1)} %get-tuple-element.73), channel_id=1, source_target_pairs={{0,8},{8,16},{16,24},{1,9},{9,17},{17,25},{2,10},{10,18},{18,26},{... | collective-permute-start | bytes 393224 | tf_op jit(solution)/shard_map/ppermute | solution.py:15
  421.1 29.8 %collective-permute-start.11 = (bf16[64,144,8]{1,2,0:T(8,128)(2,1)}, bf16[64,144,8]{1,2,0:T(8,128)(2,1)}, u32[]{:S(2)}, u32[]{:S(2)}) collective-permute-start(bf16[64,144,8]{1,2,0:T(8,128)(2,1)} %copy.99), channel_id=1, source_target_pairs={{2,0},{4,2},{6,4},{3,1},{5,3},{7,5},{10,8},{12,10},{14,12},{11,9},... | collective-permute-start | bytes 442376 | tf_op jit(solution)/shard_map/ppermute | solution.py:18
  427.0 29.0 %collective-permute-start.10 = (bf16[64,144,8]{1,2,0:T(8,128)(2,1)}, bf16[64,144,8]{1,2,0:T(8,128)(2,1)}, u32[]{:S(2)}, u32[]{:S(2)}) collective-permute-start(bf16[64,144,8]{1,2,0:T(8,128)(2,1)} %copy.98), channel_id=1, source_target_pairs={{0,2},{2,4},{4,6},{1,3},{3,5},{5,7},{8,10},{10,12},{12,14},{9,11},... | collective-permute-start | bytes 442376 | tf_op jit(solution)/shard_map/ppermute | solution.py:15
  439.7 83.8 %collective-permute-start.15 = (bf16[64,144,8]{1,2,0:T(8,128)(2,1)S(1)}, bf16[64,144,8]{1,2,0:T(8,128)(2,1)S(1)}, u32[]{:S(2)}, u32[]{:S(2)}) collective-permute-start(bf16[64,144,8]{1,2,0:T(8,128)(2,1)S(1)} %copy.104), channel_id=1, source_target_pairs={{2,0},{4,2},{6,4},{3,1},{5,3},{7,5},{10,8},{12,10},{14,12},{11,9},... | collective-permute-start | bytes 442376 | tf_op jit(solution)/shard_map/ppermute | solution.py:18
  445.6 82.1 %collective-permute-start.14 = (bf16[64,144,8]{1,2,0:T(8,128)(2,1)}, bf16[64,144,8]{1,2,0:T(8,128)(2,1)}, u32[]{:S(2)}, u32[]{:S(2)}) collective-permute-start(bf16[64,144,8]{1,2,0:T(8,128)(2,1)} %copy.103), channel_id=1, source_target_pairs={{0,2},{2,4},{4,6},{1,3},{3,5},{5,7},{8,10},{10,12},{12,14},{9,11},... | collective-permute-start | bytes 442376 | tf_op jit(solution)/shard_map/ppermute | solution.py:15
  461.0 7.8 %copy-start.10 = (bf16[1,64,128,128]{3,2,1,0:T(8,128)(2,1)S(1)}, bf16[1,64,128,128]{3,2,1,0:T(8,128)(2,1)}, u32[]{:S(2)}) copy-start(bf16[1,64,128,128]{3,2,1,0:T(8,128)(2,1)} %param.10) | copy-start | bytes 6291460
  468.8 2.1 copy-start
  494.2 4.8 copy-start.1
  494.2 8.3 %copy-start.11 = (bf16[1,64,128,128]{3,2,1,0:T(8,128)(2,1)S(1)}, bf16[1,64,128,128]{3,2,1,0:T(8,128)(2,1)}, u32[]{:S(2)}) copy-start(bf16[1,64,128,128]{3,2,1,0:T(8,128)(2,1)} %param.10) | copy-start | bytes 6291460
  494.2 8.3 %copy-start.43 = (bf16[8,128,8,128]{3,2,1,0:T(8,128)(2,1)S(1)}, bf16[8,128,8,128]{3,2,1,0:T(8,128)(2,1)}, u32[]{:S(2)}) copy-start(bf16[8,128,8,128]{3,2,1,0:T(8,128)(2,1)} %get-tuple-element.62) | copy-start | bytes 6291460
  506.5 3.7 copy-start.32
  515.0 2.2 copy-start.3
  515.0 2.2 copy-start.52
  523.5 17.8 %copy-start.47 = (f32[9,64,64]{2,1,0:T(8,128)}, f32[9,64,64]{2,1,0:T(8,128)S(1)}, u32[]{:S(2)}) copy-start(f32[9,64,64]{2,1,0:T(8,128)S(1)} %fusion.233) | copy-start | bytes 442372
  565.1 3.7 copy-start.18
  572.0 2.2 copy-start.6
  572.0 2.9 copy-start.25
  576.5 1.6 copy-start.23
  579.7 1.6 copy-start.22
  582.9 1.6 copy-start.20
  584.5 1.6 copy-start.19
  586.1 2.2 copy-start.12
  586.1 2.2 copy-start.50
  586.1 2.2 copy-start.54
  588.3 4.1 copy-start.55
  588.3 4.1 copy-start.58
  (17 other events, 27.1 us)
Sparse Core Ops, SparseCore 0:
  565.2 125.7 all-reduce.6
where the time goes:
time: 712 us; the launch traced here: 702 us
  local copies, waits for them, and re-layouts  212 us (30%)
  blocking collectives  148 us (21%)
  waiting for transfers between devices  97.1 us (14%)
  matrix products  93.4 us (13%)
  other arithmetic  68.4 us (10%)
  starting transfers between devices  59.9 us (8%)
  between operations  22.4 us (3%)
    unnamed x129, local copies, waits for them, and re-layouts  113 us
    psum x3, blocking collectives, paired_total(): return lax.psum((first, second), ('row', 'col'))  110 us
    psum x1, waiting for transfers between devices, local(): lax.psum((grad_one, grad_two, grad_g_one, grad_g_two, grad_int, loss), ('...  60.8 us
    psum x1, blocking collectives, local(): lax.psum((grad_one, grad_two, grad_g_one, grad_g_two, grad_int, loss), ('...  37.8 us
    dot_general x18, matrix products, convolve_backward(): jnp.dot(kernel_weights[step].T, window_slice.reshape(chans, -1), preferre...  37.6 us
    concatenate x8, other arithmetic, padded(): block = jnp.concatenate([low, block, high], axis=dim)  34.8 us
    ppermute x8, starting transfers between devices, padded(): lax.ppermute(lax.slice_in_dim(block, block.shape[dim] - width, None, axis...  33.8 us
    dot_general x18, matrix products, kernel_weight_gradient(): lax.dot_general(flat, window_slice.reshape(chans, -1), (((1,), (1,)), (()...  30.2 us
  transfers between devices with their start and end apart: 20, of which 4 were waited for; matrix products, arithmetic and copies ran while one was open for 30% of the time, Pallas kernels for 0%

commit v1 on v0

--- a/solution.py
+++ b/solution.py
@@ -5,6 +5,11 @@
 
 kernel_reach = 8
 eps = 1e-05
+
+
+def axis_by_axis(value, one, other):
+    inner = lax.psum(value, one)
+    return lax.psum(inner, other)
 
 
 def padded(block, sides, width):
@@ -100,7 +105,7 @@
 
 
 def paired_total(first, second):
-    return lax.psum((first, second), ("row", "col"))
+    return axis_by_axis((first, second), "col", "row")
 
 
 def normalize(values, count):

time: 712 us -> 666 us (0.935)
  blocking collectives: 148 us -> 102 us
    psum x3 -> x6, blocking collectives: 110 us -> 63.3 us  [the longest x3 46.1 us: axis_by_axis(): inner = lax.psum(value, one)]
  transfers between devices with their start and end apart: 20 -> 20, of which waited for: 4 -> 4; matrix products, arithmetic and copies ran while one was open for 30% -> 32% of each run, Pallas kernels for 0% -> 0%
where the time goes in v1:
time: 666 us; the launch traced here: 656 us
  local copies, waits for them, and re-layouts  212 us (32%)
  blocking collectives  102 us (15%)
  waiting for transfers between devices  97.2 us (15%)
  matrix products  93.3 us (14%)
  other arithmetic  68.5 us (10%)
  starting transfers between devices  60.5 us (9%)
  between operations  22.4 us (3%)
    unnamed x129, local copies, waits for them, and re-layouts  113 us
    psum x1, waiting for transfers between devices, local(): lax.psum((grad_one, grad_two, grad_g_one, grad_g_two, grad_int, loss), ('...  60.9 us
    psum x3, blocking collectives, axis_by_axis(): inner = lax.psum(value, one)  46.1 us
    psum x1, blocking collectives, local(): lax.psum((grad_one, grad_two, grad_g_one, grad_g_two, grad_int, loss), ('...  38.2 us
    dot_general x18, matrix products, convolve_backward(): jnp.dot(kernel_weights[step].T, window_slice.reshape(chans, -1), preferre...  37.6 us
    concatenate x8, other arithmetic, padded(): block = jnp.concatenate([low, block, high], axis=dim)  34.8 us
    ppermute x8, starting transfers between devices, padded(): lax.ppermute(lax.slice_in_dim(block, block.shape[dim] - width, None, axis...  34.3 us
    dot_general x18, matrix products, kernel_weight_gradient(): lax.dot_general(flat, window_slice.reshape(chans, -1), (((1,), (1,)), (()...  30.2 us
  transfers between devices with their start and end apart: 20, of which 4 were waited for; matrix products, arithmetic and copies ran while one was open for 32% of the time, Pallas kernels for 0%

profile of v1, /device:TPU:0, one launch (start us, length us, event | category | flops | bytes accessed | tf_op | source)
XLA Modules:
  0.0 655.6 jit_solution(6386728948424034810)
XLA Ops:
  7.2 4.3 copy.340
  11.5 4.6 all-to-all-start
  23.6 18.8 %all-to-all-done = bf16[1,1,64,128,128]{4,2,1,0,3:T(8,128)(2,1)} async-done(((bf16[1,1,64,128,128]{4,2,1,0,3:T(8,128)(2,1)}), bf16[1,1,64,128,128]{4,2,1,0,3:T(8,128)(2,1)}, u32[]{:S(2)}, u32[]{:S(2)}) %all-to-all-start) | async-done | bytes 2097184 | tf_op jit(solution)/shard_map/all_to_all | solution.py:126
  42.5 4.3 copy.339
  46.8 5.8 all-to-all-start.1
  52.6 4.3 fusion.4
  63.9 4.3 copy.72
  68.6 3.4 fusion.361
  72.0 3.9 copy.65
  77.3 3.9 copy.64
  81.3 5.3 collective-permute-start.2
  86.6 4.1 copy.67
  91.9 5.0 copy.66
  96.9 8.6 %pad_maximum_fusion = bf16[64,144,144]{2,0,1:T(8,128)(2,1)} fusion(bf16[64,144,8]{2,0,1:T(8,128)(2,1)} %copy.67, bf16[64,8,128]{2,0,1:T(8,128)(2,1)S(1)} %collective-permute-done.1, bf16[64,128,128]{2,0,1:T(8,128)(2,1)S(1)} %fusion.2, bf16[64,8,128]{2,0,1:T(8,128)(2,1)S(1)} %collective-permute-done, bf16[64,144,8]{2,0,1:T(8,128)(2,1)} %copy.66), kind=kLoop, calls=%fused_computation.46 | loop fusion | flops 13271040 | bytes 5308416 | tf_op jit(solution)/shard_map/concatenate | solution.py:24
  105.5 21.1 %dynamic-slice_bitcast_fusion.8 = (bf16[128,8,8,128]{3,2,1,0:T(8,128)(2,1)}, bf16[128,8,8,128]{3,2,1,0:T(8,128)(2,1)}, bf16[128,8,8,128]{3,2,1,0:T(8,128)(2,1)},...) fusion(bf16[64,144,144]{2,0,1:T(8,128)(2,1)} %pad_maximum_fusio, ...), kind=kLoop, calls=%fused_computation.182 | loop fusion | bytes 33554440
  131.0 4.6 all-to-all-start.2
  145.1 16.3 %all-to-all-done.2 = bf16[1,4,64,32,128]{4,3,2,0,1:T(8,128)(2,1)} async-done(((bf16[1,4,64,32,128]{4,3,2,0,1:T(8,128)(2,1)}), bf16[1,4,64,32,128]{4,3,2,0,1:T(8,128)(2,1)}, u32[]{:S(2)}, u32[]{:S(2)}) %all-to-all-start.2) | async-done | bytes 2097184 | tf_op jit(solution)/shard_map/all_to_all | solution.py:132
  161.3 4.1 bitcast_convert_fusion
  165.5 5.5 copy.82
  171.0 5.2 convert_reduce_fusion
  176.2 27.4 %all-reduce.4 = (f32[64]{0:T(128)S(1)}, f32[64]{0:T(128)S(1)}) all-reduce(f32[64]{0:T(128)S(1)} %get-tuple-element.14, f32[64]{0:T(128)S(1)} %get-tuple-element.13), channel_id=1, replica_groups=mesh['row'=4,'col'=4,'dp'=2] {'col'}, use_global_device_ids=true, to_apply=%region_4.0 | all-reduce | flops 128 | bytes 1024 | tf_op jit(solution)/shard_map/psum | solution.py:11
  203.5 5.7 all-reduce.7
  209.3 3.3 fusion.5
  217.0 4.3 convolution_add_fusion.26
  221.6 3.3 fusion.360
  224.9 3.9 copy.84
  230.5 3.9 copy.83
  234.4 5.3 collective-permute-start.6
  239.7 5.5 convolution_add_fusion.25
  245.2 4.2 copy.86
  249.4 5.0 copy.85
  254.4 8.7 %pad_maximum_fusion.1 = bf16[64,144,144]{2,0,1:T(8,128)(2,1)} fusion(bf16[64,144,8]{2,0,1:T(8,128)(2,1)} %copy.86, bf16[64,8,128]{2,0,1:T(8,128)(2,1)S(1)} %collective-permute-done.5, bf16[64,128,128]{2,0,1:T(8,128)(2,1)S(1)} %fusion.5, bf16[64,8,128]{2,0,1:T(8,128)(2,1)S(1)} %collective-permute-done.4, bf16[64,144,8]{2,0,1:T(8,128)(2,1)} %copy.85), kind=kLoop, calls=%fused_computation.47 | loop fusion | flops 13271040 | bytes 5308416 | tf_op jit(solution)/shard_map/concatenate | solution.py:24
  263.0 20.7 %dynamic-slice_bitcast_fusion.22 = (bf16[128,8,8,128]{3,2,1,0:T(8,128)(2,1)}, bf16[128,8,8,128]{3,2,1,0:T(8,128)(2,1)S(1)}, bf16[128,8,8,128]{3,2,1,0:T(8,128)(2...) fusion(bf16[64,144,144]{2,0,1:T(8,128)(2,1)} %pad_maximum_fusio, ...), kind=kLoop, calls=%fused_computation.211 | loop fusion | bytes 33554440
  297.1 3.4 fusion.28
  300.5 8.4 %all-reduce.3 = (f32[64]{0:T(128)S(1)}, f32[64]{0:T(128)S(1)}) all-reduce(f32[64]{0:T(128)S(1)} %get-tuple-element.10, f32[64]{0:T(128)S(1)} %get-tuple-element.9), channel_id=1, replica_groups=mesh['row'=4,'col'=4,'dp'=2] {'col'}, use_global_device_ids=true, to_apply=%region_10.11 | all-reduce | flops 128 | bytes 1024 | tf_op jit(solution)/shard_map/psum | solution.py:11
  308.9 5.6 all-reduce.6
  314.6 7.1 %multiply_reduce_fusion.1 = (f32[64]{0:T(128)}, f32[64]{0:T(128)S(1)}, f32[64]{0:T(128)S(1)}, f32[16384,64]{0,1:T(8,128)}) fusion(f32[64]{0:T(128)S(1)} %copy-done.51, f32[64]{0:T(128)S(1)} %get-tuple-element.90, f32[64]{0:T(128)S(1)} %get-tuple-element.89, f32[16384]{0:T(1024)S(1)} %fusion.247, f32[64]{0:T(128)S(1)} %copy-done.48, ...), kind=kOutput, calls=%fused_computation.80 | convolution fusion | flops 150994752 | bytes 14764800 | tf_op jit(solution)/shard_map/dot_general | solution.py:76
  321.6 10.3 %all-reduce.2 = (f32[64]{0:T(128)S(1)}, f32[64]{0:T(128)S(1)}) all-reduce(f32[64]{0:T(128)S(1)} %get-tuple-element.8, f32[64]{0:T(128)S(1)} %get-tuple-element.7), channel_id=1, replica_groups=mesh['row'=4,'col'=4,'dp'=2] {'col'}, use_global_device_ids=true, to_apply=%region_16.17 | all-reduce | flops 128 | bytes 1024 | tf_op jit(solution)/shard_map/psum | solution.py:11
  331.9 5.9 all-reduce.5
  337.8 7.4 %multiply_reduce_fusion = (f32[64]{0:T(128)}, bf16[64,16384]{1,0:T(8,128)(2,1)}, bf16[8,128,8,128]{3,2,1,0:T(8,128)(2,1)}) fusion(f32[16384]{0:T(1024)S(1)} %fusion.247, f32[64]{0:T(128)S(1)} %get-tuple-element.97, f32[64]{0:T(128)S(1)} %get-tuple-element.98, f32[64]{0:T(128)S(1)} %get-tuple-element.90, f32[64]{0:T(128)S(1)} %get-tuple-element.89, ...), kind=kLoop, calls=%fused_computation.79 | loop fusion | flops 20971456 | bytes 12650240 | tf_op jit(solution)/shard_map/reduce_sum | solution.py:170
  362.7 4.0 collective-permute-start.12
  367.1 3.3 fusion.359
  370.4 4.6 copy.99
  376.2 4.5 copy.98
  380.8 5.3 collective-permute-start.10
  386.3 3.3 fusion.358
  389.6 3.9 copy.104
  394.8 4.6 copy.103
  399.4 5.4 collective-permute-start.14
  404.8 5.0 copy.101
  409.8 5.0 copy.100
  414.8 7.7 %pad_maximum_fusion.2 = bf16[64,144,144]{2,0,1:T(8,128)(2,1)S(1)} fusion(bf16[64,144,8]{2,0,1:T(8,128)(2,1)} %copy.101, bf16[64,8,128]{2,0,1:T(8,128)(2,1)S(1)} %collective-permute-done.9, bf16[64,128,128]{2,0,1:T(8,128)(2,1)} %copy-done.7, bf16[64,8,128]{2,0,1:T(8,128)(2,1)S(1)} %collective-permute-done.8, bf16[64,144,8]{2,0,1:T(8,128)(2,1)} %copy.100), kind=kLoop, calls=%fused_computation.48 | loop fusion | flops 13271040 | bytes 5308416 | tf_op jit(solution)/shard_map/concatenate | solution.py:24
  426.5 21.5 %dynamic-slice_bitcast_fusion.16 = (bf16[128,8,8,128]{3,2,1,0:T(8,128)(2,1)}, bf16[128,8,8,128]{3,2,1,0:T(8,128)(2,1)}, bf16[128,8,8,128]{3,2,1,0:T(8,128)(2,1)}...) fusion(bf16[64,144,144]{2,0,1:T(8,128)(2,1)} %copy-done, ...), kind=kLoop, calls=%fused_computation.191 | loop fusion | bytes 33554440
  448.0 4.7 fusion.155
  452.7 3.5 fusion.215
  471.0 4.4 convolution_add_fusion.4
  477.3 4.1 copy.106
  481.4 5.0 copy.105
  486.4 8.6 %pad_maximum_fusion.3 = bf16[64,144,144]{2,0,1:T(8,128)(2,1)} fusion(bf16[64,144,8]{2,0,1:T(8,128)(2,1)} %copy.106, bf16[64,8,128]{2,0,1:T(8,128)(2,1)S(1)} %collective-permute-done.13, bf16[64,128,128]{2,0,1:T(8,128)(2,1)S(1)} %get-tuple-element.70, bf16[64,8,128]{2,0,1:T(8,128)(2,1)S(1)} %collective-permute-done.12, bf16[64,144,8]{2,0,1:T(8,128)(2,1)} %copy.105), kind=kLoop, calls=%fused_computation.49 | loop fusion | flops 13271040 | bytes 5308416 | tf_op jit(solution)/shard_map/concatenate | solution.py:24
  495.0 20.9 %dynamic-slice_bitcast_fusion = (bf16[128,8,8,128]{3,2,1,0:T(8,128)(2,1)}, bf16[128,8,8,128]{3,2,1,0:T(8,128)(2,1)}, bf16[128,8,8,128]{3,2,1,0:T(8,128)(2,1)}, b...) fusion(bf16[64,144,144]{2,0,1:T(8,128)(2,1)} %pad_maximum_fusio, ...), kind=kLoop, calls=%fused_computation.173 | loop fusion | bytes 33554440
  518.8 3.6 convolution_add_fusion.3
  542.0 3.4 fusion.3
  546.0 38.2 %all-reduce = (f32[64]{0:T(128)}, f32[64]{0:T(128)}, f32[64]{0:T(128)}, f32[]{:T(128)}) all-reduce(f32[64]{0:T(128)S(1)} %get-tuple-element.12, f32[64]{0:T(128)S(1)} %copy-done.58, f32[64]{0:T(128)S(1)} %copy-done.55, f32[]{:T(128)S(6)} %div.41), channel_id=1, replica_groups=mesh['row'=4,'col'=4,'dp'=2] {'row','col','dp'}, use_global_device_ids=true, to_apply=%region_21.22 | all-reduce | flops 193 | bytes 1544 | tf_op jit(solution)/shard_map/psum | solution.py:175
  584.3 60.9 %all-reduce.10.cloned.1.call-done = (f32[9,64,64]{2,1,0:T(8,128)}, f32[9,64,64]{2,1,0:T(8,128)}) async-done(((f32[9,64,64]{2,1,0:T(8,128)}, f32[9,64,64]{2,1,0:T(8,128)}), (f32[9,64,64]{2,1,0:T(8,128)}, f32[9,64,64]{2,1,0:T(8,128)})) %all-reduce.10.cloned.1.call-update) | async-done | bytes 294928 | tf_op jit(solution)/shard_map/psum | solution.py:175
  (219 shorter events, 111.1 us)
Async XLA Ops:
  11.5 11.9 %copy-start.57 = (s32[1,512]{1,0:T(1,128)S(1)}, s32[1,512]{1,0:T(1,128)}, u32[]{:S(2)}) copy-start(s32[1,512]{1,0:T(1,128)} %param.11) | copy-start | bytes 6148
  11.5 31.0 %all-to-all-start = ((bf16[1,1,64,128,128]{4,2,1,0,3:T(8,128)(2,1)}), bf16[1,1,64,128,128]{4,2,1,0,3:T(8,128)(2,1)}, u32[]{:S(2)}, u32[]{:S(2)}) async-start(bf16[1,1,64,128,128]{4,2,1,0,3:T(8,128)(2,1)} %bitcast.515), calls=%async_computation | async-start | bytes 4194304 | tf_op jit(solution)/shard_map/all_to_all | solution.py:126
  19.0 49.2 %collective-permute-start.1 = (bf16[64,8,128]{2,0,1:T(8,128)(2,1)S(1)}, bf16[64,8,128]{2,0,1:T(8,128)(2,1)S(1)}, u32[]{:S(2)}, u32[]{:S(2)}) collective-permute-start(bf16[64,8,128]{2,0,1:T(8,128)(2,1)S(1)} %get-tuple-element.86), channel_id=1, source_target_pairs={{8,0},{16,8},{24,16},{9,1},{17,9},{25,17},{10,2},{18,10},{26,18},{... | collective-permute-start | bytes 393224 | tf_op jit(solution)/shard_map/ppermute | solution.py:23
  20.3 47.9 %collective-permute-start = (bf16[64,8,128]{2,0,1:T(8,128)(2,1)S(1)}, bf16[64,8,128]{2,0,1:T(8,128)(2,1)S(1)}, u32[]{:S(2)}, u32[]{:S(2)}) collective-permute-start(bf16[64,8,128]{2,0,1:T(8,128)(2,1)S(1)} %get-tuple-element.85), channel_id=1, source_target_pairs={{0,8},{8,16},{16,24},{1,9},{9,17},{17,25},{2,10},{10,18},{18,26},{... | collective-permute-start | bytes 393224 | tf_op jit(solution)/shard_map/ppermute | solution.py:20
  46.8 10.1 %copy-start.56 = (s32[2]{0:T(128)S(1)}, s32[2]{0:T(128)}, u32[]{:S(2)}) copy-start(s32[2]{0:T(128)} %param.12) | copy-start | bytes 28
  46.8 84.2 %all-to-all-start.1 = ((bf16[4,1,64,32,128]{4,3,2,1,0:T(8,128)(2,1)}), bf16[4,1,64,32,128]{4,3,2,1,0:T(8,128)(2,1)}, u32[]{:S(2)}, u32[]{:S(2)}) async-start(bf16[4,1,64,32,128]{4,3,2,1,0:T(8,128)(2,1)} %bitcast.520), calls=%async_computation.1 | async-start | bytes 4194304 | tf_op jit(solution)/shard_map/all_to_all | solution.py:125
  75.9 10.7 %collective-permute-start.3 = (bf16[64,144,8]{1,2,0:T(8,128)(2,1)S(1)}, bf16[64,144,8]{1,2,0:T(8,128)(2,1)S(1)}, u32[]{:S(2)}, u32[]{:S(2)}) collective-permute-start(bf16[64,144,8]{1,2,0:T(8,128)(2,1)S(1)} %copy.65), channel_id=1, source_target_pairs={{2,0},{4,2},{6,4},{3,1},{5,3},{7,5},{10,8},{12,10},{14,12},{11,9},... | collective-permute-start | bytes 442376 | tf_op jit(solution)/shard_map/ppermute | solution.py:23
  81.3 10.7 %collective-permute-start.2 = (bf16[64,144,8]{1,2,0:T(8,128)(2,1)S(1)}, bf16[64,144,8]{1,2,0:T(8,128)(2,1)}, u32[]{:S(2)}, u32[]{:S(2)}) collective-permute-start(bf16[64,144,8]{1,2,0:T(8,128)(2,1)S(1)} %copy.64), channel_id=1, source_target_pairs={{0,2},{2,4},{4,6},{1,3},{3,5},{5,7},{8,10},{10,12},{12,14},{9,11},... | collective-permute-start | bytes 442376 | tf_op jit(solution)/shard_map/ppermute | solution.py:20
  105.5 21.1 %copy-start.44 = (bf16[9,64,64]{2,1,0:T(8,128)(2,1)S(1)}, bf16[9,64,64]{2,1,0:T(8,128)(2,1)}, u32[]{:S(2)}) copy-start(bf16[9,64,64]{2,1,0:T(8,128)(2,1)} %param.14) | copy-start | bytes 221188
  131.0 4.9 copy-start.29
  131.0 30.3 %all-to-all-start.2 = ((bf16[1,4,64,32,128]{4,3,2,0,1:T(8,128)(2,1)}), bf16[1,4,64,32,128]{4,3,2,0,1:T(8,128)(2,1)}, u32[]{:S(2)}, u32[]{:S(2)}) async-start(bf16[1,4,64,32,128]{4,3,2,0,1:T(8,128)(2,1)} %bitcast.21), calls=%async_computation.2 | async-start | bytes 4194304 | tf_op jit(solution)/shard_map/all_to_all | solution.py:132
  135.6 509.6 %all-reduce.10.cloned.1.call-start = ((), (), s32[]{:S(2)}) async-start(), calls=%async_computation.3 | async-start | bytes 1179648 | tf_op jit(solution)/shard_map/psum | solution.py:175
  135.8 3.1 copy-start.27
  140.5 1.7 copy-start.26
  165.5 5.5 copy-start.39
  171.0 38.3 %copy-start.53 = (f32[64]{0:T(128)S(1)}, f32[64]{0:T(128)}, u32[]{:S(2)}) copy-start(f32[64]{0:T(128)} %param.15) | copy-start | bytes 772
  209.3 7.7 %copy-start.14 = (f32[16384,64]{0,1:T(8,128)S(1)}, f32[16384,64]{0,1:T(8,128)}, u32[]{:S(2)}) copy-start(f32[16384,64]{0,1:T(8,128)} %convolution_add_fusion.27) | copy-start | bytes 12582916
  209.3 80.8 %copy-start.49 = (f32[64]{0:T(128)}, f32[64]{0:T(128)S(1)}, u32[]{:S(2)}) copy-start(f32[64]{0:T(128)S(1)} %get-tuple-element.94) | copy-start | bytes 772
  212.6 41.8 %copy-start.4 = (bf16[64,128,128]{2,0,1:T(8,128)(2,1)}, bf16[64,128,128]{2,0,1:T(8,128)(2,1)S(1)}, u32[]{:S(2)}) copy-start(bf16[64,128,128]{2,0,1:T(8,128)(2,1)S(1)} %fusion.5) | copy-start | bytes 6291460
  212.7 8.7 %collective-permute-start.5 = (bf16[64,8,128]{2,0,1:T(8,128)(2,1)S(1)}, bf16[64,8,128]{2,0,1:T(8,128)(2,1)S(1)}, u32[]{:S(2)}, u32[]{:S(2)}) collective-permute-start(bf16[64,8,128]{2,0,1:T(8,128)(2,1)S(1)} %get-tuple-element.84), channel_id=1, source_target_pairs={{8,0},{16,8},{24,16},{9,1},{17,9},{25,17},{10,2},{18,10},{26,18},{... | collective-permute-start | bytes 393224 | tf_op jit(solution)/shard_map/ppermute | solution.py:23
  214.0 7.4 %collective-permute-start.4 = (bf16[64,8,128]{2,0,1:T(8,128)(2,1)S(1)}, bf16[64,8,128]{2,0,1:T(8,128)(2,1)S(1)}, u32[]{:S(2)}, u32[]{:S(2)}) collective-permute-start(bf16[64,8,128]{2,0,1:T(8,128)(2,1)S(1)} %get-tuple-element.83), channel_id=1, source_target_pairs={{0,8},{8,16},{16,24},{1,9},{9,17},{17,25},{2,10},{10,18},{18,26},{... | collective-permute-start | bytes 393224 | tf_op jit(solution)/shard_map/ppermute | solution.py:20
  228.8 16.4 %collective-permute-start.7 = (bf16[64,144,8]{1,2,0:T(8,128)(2,1)S(1)}, bf16[64,144,8]{1,2,0:T(8,128)(2,1)S(1)}, u32[]{:S(2)}, u32[]{:S(2)}) collective-permute-start(bf16[64,144,8]{1,2,0:T(8,128)(2,1)S(1)} %copy.84), channel_id=1, source_target_pairs={{2,0},{4,2},{6,4},{3,1},{5,3},{7,5},{10,8},{12,10},{14,12},{11,9},... | collective-permute-start | bytes 442376 | tf_op jit(solution)/shard_map/ppermute | solution.py:23
  234.4 15.0 %collective-permute-start.6 = (bf16[64,144,8]{1,2,0:T(8,128)(2,1)S(1)}, bf16[64,144,8]{1,2,0:T(8,128)(2,1)}, u32[]{:S(2)}, u32[]{:S(2)}) collective-permute-start(bf16[64,144,8]{1,2,0:T(8,128)(2,1)S(1)} %copy.83), channel_id=1, source_target_pairs={{0,2},{2,4},{4,6},{1,3},{3,5},{5,7},{8,10},{10,12},{12,14},{9,11},... | collective-permute-start | bytes 442376 | tf_op jit(solution)/shard_map/ppermute | solution.py:20
  263.0 20.7 %copy-start.45 = (bf16[9,64,64]{2,1,0:T(8,128)(2,1)S(1)}, bf16[9,64,64]{2,1,0:T(8,128)(2,1)}, u32[]{:S(2)}) copy-start(bf16[9,64,64]{2,1,0:T(8,128)(2,1)} %param.13) | copy-start | bytes 221188
  283.8 2.4 copy-start.38
  291.0 2.2 copy-start.34
  297.1 17.4 %copy-start.42 = (bf16[128,8,8,128]{3,2,1,0:T(8,128)(2,1)S(1)}, bf16[128,8,8,128]{3,2,1,0:T(8,128)(2,1)}, u32[]{:S(2)}) copy-start(bf16[128,8,8,128]{3,2,1,0:T(8,128)(2,1)} %get-tuple-element.60) | copy-start | bytes 6291460
  297.1 17.4 %copy-start.51 = (f32[64]{0:T(128)S(1)}, f32[64]{0:T(128)}, u32[]{:S(2)}) copy-start(f32[64]{0:T(128)} %param.16) | copy-start | bytes 772
  337.8 7.4 %copy-start.2 = (f32[16384,64]{0,1:T(8,128)S(1)}, f32[16384,64]{0,1:T(8,128)}, u32[]{:S(2)}) copy-start(f32[16384,64]{0,1:T(8,128)} %get-tuple-element.95) | copy-start | bytes 12582916
  337.8 7.4 %copy-start.15 = (f32[16384,64]{0,1:T(8,128)S(1)}, f32[16384,64]{0,1:T(8,128)}, u32[]{:S(2)}) copy-start(f32[16384,64]{0,1:T(8,128)} %get-tuple-element.96) | copy-start | bytes 12582916
  337.8 10.4 %slice-start = ((s8[4718592]{0:T(1024)(128)(4,1)}), s8[524288]{0:T(1024)(128)(4,1)S(1)}, s32[]{:S(2)}) async-start(s8[4718592]{0:T(1024)(128)(4,1)} %bitcast.516), calls=%async_computation.4 | async-start | bytes 1048576
  345.2 3.0 slice-start.1
  348.2 18.6 %copy-start.7 = (bf16[64,128,128]{2,0,1:T(8,128)(2,1)}, bf16[64,128,128]{2,0,1:T(8,128)(2,1)S(1)}, u32[]{:S(2)}) copy-start(bf16[64,128,128]{2,0,1:T(8,128)(2,1)S(1)} %get-tuple-element.69) | copy-start | bytes 6291460
  350.2 2.0 copy-start.5
  357.0 13.4 %copy-start.46 = (f32[9,64,64]{2,1,0:T(8,128)}, f32[9,64,64]{2,1,0:T(8,128)S(1)}, u32[]{:S(2)}) copy-start(f32[9,64,64]{2,1,0:T(8,128)S(1)} %fusion.197) | copy-start | bytes 442372
  357.1 9.7 %collective-permute-start.9 = (bf16[64,8,128]{2,0,1:T(8,128)(2,1)S(1)}, bf16[64,8,128]{2,0,1:T(8,128)(2,1)S(1)}, u32[]{:S(2)}, u32[]{:S(2)}) collective-permute-start(bf16[64,8,128]{2,0,1:T(8,128)(2,1)S(1)} %get-tuple-element.82), channel_id=1, source_target_pairs={{8,0},{16,8},{24,16},{9,1},{17,9},{25,17},{10,2},{18,10},{26,18},{... | collective-permute-start | bytes 393224 | tf_op jit(solution)/shard_map/ppermute | solution.py:23
  358.4 8.4 %collective-permute-start.8 = (bf16[64,8,128]{2,0,1:T(8,128)(2,1)S(1)}, bf16[64,8,128]{2,0,1:T(8,128)(2,1)S(1)}, u32[]{:S(2)}, u32[]{:S(2)}) collective-permute-start(bf16[64,8,128]{2,0,1:T(8,128)(2,1)S(1)} %get-tuple-element.81), channel_id=1, source_target_pairs={{0,8},{8,16},{16,24},{1,9},{9,17},{17,25},{2,10},{10,18},{18,26},{... | collective-permute-start | bytes 393224 | tf_op jit(solution)/shard_map/ppermute | solution.py:20
  361.4 24.6 %collective-permute-start.13 = (bf16[64,8,128]{2,0,1:T(8,128)(2,1)S(1)}, bf16[64,8,128]{2,0,1:T(8,128)(2,1)S(1)}, u32[]{:S(2)}, u32[]{:S(2)}) collective-permute-start(bf16[64,8,128]{2,0,1:T(8,128)(2,1)S(1)} %get-tuple-element.80), channel_id=1, source_target_pairs={{8,0},{16,8},{24,16},{9,1},{17,9},{25,17},{10,2},{18,10},{26,18},{... | collective-permute-start | bytes 393224 | tf_op jit(solution)/shard_map/ppermute | solution.py:23
  362.7 23.3 %collective-permute-start.12 = (bf16[64,8,128]{2,0,1:T(8,128)(2,1)S(1)}, bf16[64,8,128]{2,0,1:T(8,128)(2,1)S(1)}, u32[]{:S(2)}, u32[]{:S(2)}) collective-permute-start(bf16[64,8,128]{2,0,1:T(8,128)(2,1)S(1)} %get-tuple-element.79), channel_id=1, source_target_pairs={{0,8},{8,16},{16,24},{1,9},{9,17},{17,25},{2,10},{10,18},{18,26},{... | collective-permute-start | bytes 393224 | tf_op jit(solution)/shard_map/ppermute | solution.py:20
  374.9 29.8 %collective-permute-start.11 = (bf16[64,144,8]{1,2,0:T(8,128)(2,1)}, bf16[64,144,8]{1,2,0:T(8,128)(2,1)}, u32[]{:S(2)}, u32[]{:S(2)}) collective-permute-start(bf16[64,144,8]{1,2,0:T(8,128)(2,1)} %copy.99), channel_id=1, source_target_pairs={{2,0},{4,2},{6,4},{3,1},{5,3},{7,5},{10,8},{12,10},{14,12},{11,9},... | collective-permute-start | bytes 442376 | tf_op jit(solution)/shard_map/ppermute | solution.py:23
  380.8 29.0 %collective-permute-start.10 = (bf16[64,144,8]{1,2,0:T(8,128)(2,1)}, bf16[64,144,8]{1,2,0:T(8,128)(2,1)}, u32[]{:S(2)}, u32[]{:S(2)}) collective-permute-start(bf16[64,144,8]{1,2,0:T(8,128)(2,1)} %copy.98), channel_id=1, source_target_pairs={{0,2},{2,4},{4,6},{1,3},{3,5},{5,7},{8,10},{10,12},{12,14},{9,11},... | collective-permute-start | bytes 442376 | tf_op jit(solution)/shard_map/ppermute | solution.py:20
  393.5 83.8 %collective-permute-start.15 = (bf16[64,144,8]{1,2,0:T(8,128)(2,1)S(1)}, bf16[64,144,8]{1,2,0:T(8,128)(2,1)S(1)}, u32[]{:S(2)}, u32[]{:S(2)}) collective-permute-start(bf16[64,144,8]{1,2,0:T(8,128)(2,1)S(1)} %copy.104), channel_id=1, source_target_pairs={{2,0},{4,2},{6,4},{3,1},{5,3},{7,5},{10,8},{12,10},{14,12},{11,9},... | collective-permute-start | bytes 442376 | tf_op jit(solution)/shard_map/ppermute | solution.py:23
  399.4 82.1 %collective-permute-start.14 = (bf16[64,144,8]{1,2,0:T(8,128)(2,1)}, bf16[64,144,8]{1,2,0:T(8,128)(2,1)}, u32[]{:S(2)}, u32[]{:S(2)}) collective-permute-start(bf16[64,144,8]{1,2,0:T(8,128)(2,1)} %copy.103), channel_id=1, source_target_pairs={{0,2},{2,4},{4,6},{1,3},{3,5},{5,7},{8,10},{10,12},{12,14},{9,11},... | collective-permute-start | bytes 442376 | tf_op jit(solution)/shard_map/ppermute | solution.py:20
  414.8 7.8 %copy-start.10 = (bf16[1,64,128,128]{3,2,1,0:T(8,128)(2,1)S(1)}, bf16[1,64,128,128]{3,2,1,0:T(8,128)(2,1)}, u32[]{:S(2)}) copy-start(bf16[1,64,128,128]{3,2,1,0:T(8,128)(2,1)} %param.10) | copy-start | bytes 6291460
  422.6 2.1 copy-start
  448.0 4.8 copy-start.1
  448.0 8.3 %copy-start.11 = (bf16[1,64,128,128]{3,2,1,0:T(8,128)(2,1)S(1)}, bf16[1,64,128,128]{3,2,1,0:T(8,128)(2,1)}, u32[]{:S(2)}) copy-start(bf16[1,64,128,128]{3,2,1,0:T(8,128)(2,1)} %param.10) | copy-start | bytes 6291460
  448.0 8.3 %copy-start.43 = (bf16[8,128,8,128]{3,2,1,0:T(8,128)(2,1)S(1)}, bf16[8,128,8,128]{3,2,1,0:T(8,128)(2,1)}, u32[]{:S(2)}) copy-start(bf16[8,128,8,128]{3,2,1,0:T(8,128)(2,1)} %get-tuple-element.68) | copy-start | bytes 6291460
  460.3 3.7 copy-start.32
  468.8 2.2 copy-start.3
  468.8 2.2 copy-start.52
  477.3 17.8 %copy-start.47 = (f32[9,64,64]{2,1,0:T(8,128)}, f32[9,64,64]{2,1,0:T(8,128)S(1)}, u32[]{:S(2)}) copy-start(f32[9,64,64]{2,1,0:T(8,128)S(1)} %fusion.233) | copy-start | bytes 442372
  518.7 3.7 copy-start.18
  522.4 1.6 copy-start.17
  525.6 2.2 copy-start.6
  525.6 2.9 copy-start.25
  533.3 1.6 copy-start.22
  536.5 1.6 copy-start.20
  538.1 1.6 copy-start.19
  539.7 2.2 copy-start.12
  539.7 2.2 copy-start.50
  539.7 2.2 copy-start.54
  542.0 4.1 copy-start.55
  542.0 4.1 copy-start.58
  (17 other events, 27.1 us)
Sparse Core Ops, SparseCore 0:
  518.9 126.2 all-reduce.9
